TPU v7x, 32 devices: a whole 2x2x4 slice. The times are simulated.
32 devices in a mesh: groups: 2 (over y), layer: 4 (over z), dp: 2 (over x), chan: 2 (over core).
Axes of the slice: x: 2, y: 2, z: 4, core: 2. Of those that a mesh axis runs over, the one named last changes fastest.
Arguments:
- activations: bfloat16 [4, 4, 32, 16, 16, 128], P('layer', None, ('groups', 'dp', 'chan')), parts along dimension 2, may hold values from -0.94921875 to 0.94921875
- weights: bfloat16 [4, 4, 9, 128, 128], P('layer'), may hold values from -0.1875 to 0.1875
- guesses: bfloat16 [4, 32, 16, 16, 128], P('layer', ('groups', 'dp', 'chan')), parts along dimension 1, may hold values from -6 to 6
- terminal: bfloat16 [32, 16, 16, 128], P(('groups', 'dp', 'chan')), parts along dimension 0, may hold values from -6 to 6
- coarse_rates: float32 [4, 128], P('layer'), may hold values from 0.0074 to 1, as said below
- block_layers: int32 [4], P('layer'), may hold values from 1 to 4, 12 in all
Outputs:
- corrected: bfloat16 [4, 32, 16, 16, 128], P('layer', ('groups', 'dp', 'chan')), parts along dimension 1
- kernel_grads: bfloat16 [8, 4, 9, 128, 128], P(('groups', 'layer')), parts along dimension 0
There are 2 independent parts, one for each index of `groups`. A program takes and returns all parts, laid end to end along the dimension named above; an argument that names none is the same for every part. Nothing has to cross between parts.
Inputs may be any that keep to these rules, and one draw needn't show every extreme that they name: `block_layers`: every block holds at least one layer and some block holds exactly 4; the counts sum to 12. `coarse_rates`: strictly positive.
All inputs are finite; a program needn't handle non-finite values.
Results may differ from a plain program's by a relative error of at most 0.0055.
Values may be sent and summed in bfloat16 or wider, within the bound.
A program may use at most 64 MiB of HBM per device.

v0:
```python
import jax
import jax.numpy as jnp
from jax import lax
from jax.sharding import PartitionSpec as P

MMAX = 4
step_size = 0.25
OFFSETS = [(row_off, col_off) for row_off in (-1, 0, 1) for col_off in (-1, 0, 1)]


def shifted(value, axis, steps):
    count = lax.axis_size(axis)
    first, last = (max(0, -steps), min(count, count - steps))
    return lax.ppermute(value, axis, [(source, source + steps) for source in range(first, last)])


def entering(part, axis, combine, identity):
    count = lax.axis_size(axis)
    place = lax.axis_index(axis)
    ahead = count - 1 - place
    gathered = jax.tree.map(lambda a: lax.all_gather(a, axis), part)
    state = jax.tree.map(lambda a, e: jnp.zeros_like(a) + jnp.asarray(e, a.dtype), part, identity)

    def one(turn, state):
        source = count - 1 - turn
        return combine(
            state, jax.tree.map(lambda a: lax.dynamic_index_in_dim(a, source, 0, False), gathered)
        )

    return lax.fori_loop(0, ahead, one, state)


def adjoint_step(adjoint, activation, kernel):
    map_side = adjoint.shape[1]
    rounded = adjoint.astype(jnp.bfloat16)
    padded = jnp.pad(rounded, ((0, 0), (1, 1), (1, 1), (0, 0)))
    summed = jnp.zeros(adjoint.shape, jnp.float32)
    for index, (row_off, col_off) in enumerate(OFFSETS):
        sliced = padded[
            :, 1 - row_off : 1 - row_off + map_side, 1 - col_off : 1 - col_off + map_side, :
        ]
        summed = summed + jnp.dot(sliced, kernel[index].T, preferred_element_type=jnp.float32)
    act_float = activation.astype(jnp.float32)
    return (adjoint + step_size * (1.0 - act_float * act_float) * summed, rounded)


def kernel_grad(activation, rounded):
    map_side = rounded.shape[1]
    padded = jnp.pad(activation, ((0, 0), (1, 1), (1, 1), (0, 0)))
    pieces = []
    for row_off, col_off in OFFSETS:
        sliced = padded[
            :, 1 + row_off : 1 + row_off + map_side, 1 + col_off : 1 + col_off + map_side, :
        ]
        pieces.append(
            lax.dot_general(
                sliced,
                rounded,
                (((0, 1, 2), (0, 1, 2)), ((), ())),
                preferred_element_type=jnp.float32,
            )
        )
    return step_size * jnp.stack(pieces)


def per_device(activations, weights, guesses, terminal, coarse_rates, block_layers):
    layer_count = block_layers[0]
    acts_block = activations[0]
    kernels_block = weights[0]
    at_end = lax.axis_index("layer") == lax.axis_size("layer") - 1
    end_state = terminal.astype(jnp.float32)
    own_guess = guesses[0].astype(jnp.float32)
    received = shifted(guesses, "layer", -1)[0]
    adjoint = jnp.where(at_end, end_state, received.astype(jnp.float32))
    for slot in reversed(range(MMAX)):
        stepped, _ = adjoint_step(adjoint, acts_block[slot], kernels_block[slot])
        adjoint = jnp.where(slot < layer_count, stepped, adjoint)
    residual = adjoint - own_guess
    rates = coarse_rates[0]

    def compose(earlier, later):
        return (later[0] * earlier[0], later[1] + later[0] * earlier[1])

    identity = (jnp.ones_like(rates), jnp.zeros_like(residual))
    _, following = entering((rates, residual), "layer", compose, identity)
    correction = residual + rates * following
    corrected = (own_guess + correction).astype(jnp.bfloat16)
    received = shifted(corrected[None], "layer", -1)[0]
    adjoint = jnp.where(at_end, end_state, received.astype(jnp.float32))
    slot_list = [None] * MMAX
    for slot in reversed(range(MMAX)):
        stepped, rounded = adjoint_step(adjoint, acts_block[slot], kernels_block[slot])
        active = slot < layer_count
        slot_grad = kernel_grad(acts_block[slot], rounded)
        slot_grad = jnp.where(active, slot_grad, jnp.zeros_like(slot_grad))
        slot_list[slot] = slot_grad
        adjoint = jnp.where(active, stepped, adjoint)
    stacked = jnp.stack(slot_list)
    result = lax.psum(stacked, ("dp", "chan")).astype(jnp.bfloat16)
    return (corrected[None], result[None])


def solution(mesh):
    in_specs = (
        P("layer", None, ("groups", "dp", "chan"), None, None, None),
        P("layer", None, None, None, None),
        P("layer", ("groups", "dp", "chan"), None, None, None),
        P(("groups", "dp", "chan"), None, None, None),
        P("layer", None),
        P("layer"),
    )
    out_specs = (
        P("layer", ("groups", "dp", "chan"), None, None, None),
        P(("groups", "layer"), None, None, None, None),
    )
    return jax.shard_map(
        per_device, mesh=mesh, in_specs=in_specs, out_specs=out_specs, check_vma=False
    )
```

profile of v0, /device:TPU:0, one launch (start us, length us, event | category | flops | bytes accessed | tf_op | source)
XLA Modules:
  0.0 162.6 jit_solution(5716062791998601039)
XLA Ops:
  7.2 1.4 collective-permute-start
  9.3 9.5 %collective-permute-done = bf16[1,4,16,16,128]{4,3,2,1,0:T(8,128)(2,1)S(1)} collective-permute-done((bf16[1,4,16,16,128]{4,3,2,1,0:T(8,128)(2,1)}, bf16[1,4,16,16,128]{4,3,2,1,0:T(8,128)(2,1)S(1)}, u32[]{:S(2)}, u32[]{:S(2)}) %collective-permute-start) | collective-permute-done | bytes 262176 | tf_op jit(solution)/shard_map/ppermute | solution.py:14
  18.8 1.0 fusion.60
  19.8 1.0 fusion.63
  22.5 0.7 copy-done
  23.3 0.3 fusion.284
  25.5 0.3 fusion.285
  27.7 0.3 fusion.286
  29.9 0.5 copy-done.4
  30.4 1.1 fusion.12
  31.5 9.3 %all-gather.1 = f32[4,1,128]{2,1,0:T(1,128)S(1)} all-gather(f32[1,1,128]{2,1,0:T(1,128)S(1)} %bitcast.708), channel_id=1, replica_groups=mesh['groups'=2,'layer'=4,'dp'=2,'chan'=2] {'layer'}, dimensions={0}, use_global_device_ids=true | all-gather | bytes 2560 | tf_op jit(solution)/shard_map/all_gather | solution.py:21
  40.9 37.1 %all-gather.4.cloned.1.call-done = f32[16,16,16,128]{3,2,1,0:T(8,128)} async-done(((f32[4,16,16,128]{3,2,1,0:T(8,128)}), f32[16,16,16,128]{3,2,1,0:T(8,128)}) %all-gather.4.cloned.1.call-update) | async-done | bytes 2097168 | tf_op jit(solution)/shard_map/all_gather | solution.py:21
  78.0 3.9 %while.14 = (s32[]{:T(128)}, f32[4,16,16,128]{3,2,1,0:T(8,128)S(1)}, s32[]{:T(128)}, f32[4,4,16,16,128]{4,3,2,1,0:T(8,128)}, f32[4,128]{1,0:T(4,128)S(1)}, /*index=5*/s32[]{:T(128)}, s32[]{:T(128)}, s32[]{:T(128)}, s32[]{:T(128)}) while((s32[]{:T(128)}, f32[4,16,16,128]{3,2,1,0:T(8,128)S(1)}, s32[]{:T(128)}, f32[4,4,16,16,128]{4,3,2,1,0:T(8,128)}, ...), condition=%wide.region_1.2_spmd, body=%wide.region_0.1_spmd.sunk | while | flops 262150 | bytes 1574555 | solution.py:30
  78.1 1.3 bitcast_add_fusion.2
  79.4 1.2 bitcast_add_fusion.2
  80.7 1.2 bitcast_add_fusion.2
  82.0 1.0 fusion.62
  83.0 1.5 collective-permute-start.1
  84.7 8.3 %collective-permute-done.1 = bf16[1,4,16,16,128]{4,3,2,1,0:T(8,128)(2,1)S(1)} collective-permute-done((bf16[1,4,16,16,128]{4,3,2,1,0:T(8,128)(2,1)S(1)}, bf16[1,4,16,16,128]{4,3,2,1,0:T(8,128)(2,1)S(1)}, u32[]{:S(2)}, u32[]{:S(2)}) %collective-permute-start.1) | collective-permute-done | bytes 262176 | tf_op jit(solution)/shard_map/ppermute | solution.py:14
  94.9 0.3 fusion.287
  97.2 0.3 fusion.288
  99.4 0.3 fusion.22
  100.8 0.3 fusion.54
  101.3 0.3 fusion.52
  101.6 0.3 fusion.51
  101.9 0.3 fusion.50
  103.3 0.3 fusion.36
  103.9 0.3 fusion.34
  105.8 0.3 fusion.27
  106.4 0.3 fusion.25
  108.4 0.3 fusion.45
  110.3 45.5 %all-reduce.12 = bf16[4,9,128,128]{3,2,1,0:T(8,128)(2,1)} all-reduce(f32[4,9,128,128]{3,2,1,0:T(8,128)S(1)} %pad_maximum_fusion), channel_id=1, replica_groups=mesh['groups'=2,'layer'=4,'dp'=2,'chan'=2] {'dp','chan'}, use_global_device_ids=true, to_apply=%region_2.3 | all-reduce | flops 589824 | bytes 3538944 | tf_op jit(solution)/shard_map/psum | solution.py:99
  (105 shorter events, 21.0 us)
Async XLA Ops:
  7.2 13.7 %copy-start.3 = (bf16[1,4,9,128,128]{4,3,2,1,0:T(8,128)(2,1)S(1)}, bf16[1,4,9,128,128]{4,3,2,1,0:T(8,128)(2,1)}, u32[]{:S(2)}) copy-start(bf16[1,4,9,128,128]{4,3,2,1,0:T(8,128)(2,1)} %param.9) | copy-start | bytes 3538948
  7.2 70.8 %all-gather.4.cloned.1.call-start = ((), (), s32[]{:S(2)}) async-start(), calls=%async_computation | async-start | bytes 2621440 | tf_op jit(solution)/shard_map/all_gather | solution.py:21
  7.2 11.6 %collective-permute-start = (bf16[1,4,16,16,128]{4,3,2,1,0:T(8,128)(2,1)}, bf16[1,4,16,16,128]{4,3,2,1,0:T(8,128)(2,1)S(1)}, u32[]{:S(2)}, u32[]{:S(2)}) collective-permute-start(bf16[1,4,16,16,128]{4,3,2,1,0:T(8,128)(2,1)} %param.10), channel_id=1, source_target_pairs={{4,0},{8,4},{12,8},{5,1},{9,5},{13,9},{6,2},{10,6},{14,10},{7,3},{... | collective-permute-start | bytes 786440 | tf_op jit(solution)/shard_map/ppermute | solution.py:14
  22.0 1.2 copy-start
  22.0 1.3 copy-start.2
  29.4 1.0 copy-start.4
  30.4 1.1 copy-start.6
  78.0 3.9 %copy-start.1 = (f32[4,16,16,128]{3,2,1,0:T(8,128)S(1)}, f32[4,16,16,128]{3,2,1,0:T(8,128)}, u32[]{:S(2)}) copy-start(f32[4,16,16,128]{3,2,1,0:T(8,128)} %fusion.12) | copy-start | bytes 1572868
  83.0 10.0 %copy-start.5 = (bf16[1,4,16,16,128]{4,3,2,1,0:T(8,128)(2,1)}, bf16[1,4,16,16,128]{4,3,2,1,0:T(8,128)(2,1)S(1)}, u32[]{:S(2)}) copy-start(bf16[1,4,16,16,128]{4,3,2,1,0:T(8,128)(2,1)S(1)} %fusion.62) | copy-start | bytes 786436
  83.0 9.9 %collective-permute-start.1 = (bf16[1,4,16,16,128]{4,3,2,1,0:T(8,128)(2,1)S(1)}, bf16[1,4,16,16,128]{4,3,2,1,0:T(8,128)(2,1)S(1)}, u32[]{:S(2)}, u32[]{:S(2)}) collective-permute-start(bf16[1,4,16,16,128]{4,3,2,1,0:T(8,128)(2,1)S(1)} %fusion.62), channel_id=1, source_target_pairs={{4,0},{8,4},{12,8},{5,1},{9,5},{13,9},{6,2},{10,6},{14,10},{7,3},{... | collective-permute-start | bytes 786440 | tf_op jit(solution)/shard_map/ppermute | solution.py:14
Sparse Core Ops, SparseCore 0:
  31.6 46.3 all-gather.3
where the time goes:
time: 163 us
  waiting for transfers between devices  54.9 us (34%)
  blocking collectives  54.8 us (34%)
  matrix products  26.5 us (16%)
  between operations  15.5 us (10%)
  other arithmetic  6.39 us (4%)
  starting transfers between devices  2.93 us (2%)
    psum x1, blocking collectives, per_device(): result = lax.psum(stacked, ('dp', 'chan')).astype(jnp.bfloat16)  45.5 us
    all_gather x1, waiting for transfers between devices, entering(): gathered = jax.tree.map(lambda a: lax.all_gather(a, axis), part)  37.1 us
    ppermute x2, waiting for transfers between devices, shifted(): lax.ppermute(value, axis, [(source, source + steps) for source in range(f...  17.7 us
    dot_general x63, matrix products, adjoint_step(): jnp.dot(sliced, kernel[index].T, preferred_element_type=jnp.float32)  16.6 us
    dot_general x36, matrix products, kernel_grad(): lax.dot_general(sliced, rounded, (((0, 1, 2), (0, 1, 2)), ((), ())), pref...  9.87 us
    all_gather x1, blocking collectives, entering(): gathered = jax.tree.map(lambda a: lax.all_gather(a, axis), part)  9.34 us
    add x3, other arithmetic, compose(): return (later[0] * earlier[0], later[1] + later[0] * earlier[1])  3.78 us
  transfers between devices with their start and end apart: 3, of which 3 were waited for; matrix products, arithmetic and copies ran while one was open for 0% of the time, Pallas kernels for 0%

commit v1 on v0

--- a/solution.py
+++ b/solution.py
@@ -96,7 +96,15 @@
         slot_list[slot] = slot_grad
         adjoint = jnp.where(active, stepped, adjoint)
     stacked = jnp.stack(slot_list)
-    result = lax.psum(stacked, ("dp", "chan")).astype(jnp.bfloat16)
+
+    def _spread_vector(view):
+        a_name = "chan"
+        which_axis = "dp"
+        for pp in (a_name, which_axis):
+            view = jax.lax.psum(view, axis_name=pp)
+        return view
+
+    result = _spread_vector(stacked).astype(jnp.bfloat16)
     return (corrected[None], result[None])
 
 

time: 163 us -> 200 us (1.23)
  waiting for transfers between devices: 54.9 us -> 74.7 us
  blocking collectives: 54.8 us -> 70.1 us
    psum x0 -> x1, waiting for transfers between devices: none -> 19.9 us  [_spread_vector(): view = jax.lax.psum(view, axis_name=pp)]
    psum x1, blocking collectives: 45.5 us -> 60.8 us  [_spread_vector(): view = jax.lax.psum(view, axis_name=pp)]
  transfers between devices with their start and end apart: 3 -> 4, of which waited for: 3 -> 4; matrix products, arithmetic and copies ran while one was open for 0% -> 0% of each run, Pallas kernels for 0% -> 0%
where the time goes in v1:
time: 200 us; the launch traced here: 199 us
  waiting for transfers between devices  74.7 us (37%)
  blocking collectives  70.1 us (35%)
  matrix products  26.4 us (13%)
  between operations  15.5 us (8%)
  other arithmetic  7.79 us (4%)
  starting transfers between devices  2.98 us (1%)
    psum x1, blocking collectives, _spread_vector(): view = jax.lax.psum(view, axis_name=pp)  60.8 us
    all_gather x1, waiting for transfers between devices, entering(): gathered = jax.tree.map(lambda a: lax.all_gather(a, axis), part)  37.1 us
    psum x1, waiting for transfers between devices, _spread_vector(): view = jax.lax.psum(view, axis_name=pp)  19.9 us
    ppermute x2, waiting for transfers between devices, shifted(): lax.ppermute(value, axis, [(source, source + steps) for source in range(f...  17.7 us
    dot_general x63, matrix products, adjoint_step(): jnp.dot(sliced, kernel[index].T, preferred_element_type=jnp.float32)  16.6 us
    dot_general x36, matrix products, kernel_grad(): lax.dot_general(sliced, rounded, (((0, 1, 2), (0, 1, 2)), ((), ())), pref...  9.8 us
    all_gather x1, blocking collectives, entering(): gathered = jax.tree.map(lambda a: lax.all_gather(a, axis), part)  9.34 us
  transfers between devices with their start and end apart: 4, of which 4 were waited for; matrix products, arithmetic and copies ran while one was open for 0% of the time, Pallas kernels for 0%

profile of v1, /device:TPU:0, one launch (start us, length us, event | category | flops | bytes accessed | tf_op | source)
XLA Modules:
  0.0 199.1 jit_solution(9499280281528511257)
XLA Ops:
  7.2 1.4 collective-permute-start
  9.3 9.5 %collective-permute-done = bf16[1,4,16,16,128]{4,3,2,1,0:T(8,128)(2,1)S(1)} collective-permute-done((bf16[1,4,16,16,128]{4,3,2,1,0:T(8,128)(2,1)}, bf16[1,4,16,16,128]{4,3,2,1,0:T(8,128)(2,1)S(1)}, u32[]{:S(2)}, u32[]{:S(2)}) %collective-permute-start) | collective-permute-done | bytes 262176 | tf_op jit(solution)/shard_map/ppermute | solution.py:14
  18.8 1.0 fusion.60
  19.8 1.0 fusion.63
  22.5 0.7 copy-done
  23.3 0.3 fusion.284
  25.5 0.3 fusion.285
  27.7 0.3 fusion.286
  29.9 0.5 copy-done.4
  30.4 1.1 fusion.12
  31.6 9.3 %all-gather.1 = f32[4,1,128]{2,1,0:T(1,128)S(1)} all-gather(f32[1,1,128]{2,1,0:T(1,128)S(1)} %bitcast.708), channel_id=1, replica_groups=mesh['groups'=2,'layer'=4,'dp'=2,'chan'=2] {'layer'}, dimensions={0}, use_global_device_ids=true | all-gather | bytes 2560 | tf_op jit(solution)/shard_map/all_gather | solution.py:21
  40.9 37.1 %all-gather.4.cloned.1.call-done = f32[16,16,16,128]{3,2,1,0:T(8,128)} async-done(((f32[4,16,16,128]{3,2,1,0:T(8,128)}), f32[16,16,16,128]{3,2,1,0:T(8,128)}) %all-gather.4.cloned.1.call-update) | async-done | bytes 2097168 | tf_op jit(solution)/shard_map/all_gather | solution.py:21
  78.0 3.9 %while.14 = (s32[]{:T(128)}, f32[4,16,16,128]{3,2,1,0:T(8,128)S(1)}, s32[]{:T(128)}, f32[4,4,16,16,128]{4,3,2,1,0:T(8,128)}, f32[4,128]{1,0:T(4,128)S(1)}, /*index=5*/s32[]{:T(128)}, s32[]{:T(128)}, s32[]{:T(128)}, s32[]{:T(128)}) while((s32[]{:T(128)}, f32[4,16,16,128]{3,2,1,0:T(8,128)S(1)}, s32[]{:T(128)}, f32[4,4,16,16,128]{4,3,2,1,0:T(8,128)}, ...), condition=%wide.region_1.2_spmd, body=%wide.region_0.1_spmd.sunk | while | flops 262150 | bytes 1574555 | solution.py:30
  78.1 1.3 bitcast_add_fusion.2
  79.4 1.2 bitcast_add_fusion.2
  80.7 1.2 bitcast_add_fusion.2
  82.0 1.0 fusion.62
  83.0 1.5 collective-permute-start.1
  84.7 8.3 %collective-permute-done.1 = bf16[1,4,16,16,128]{4,3,2,1,0:T(8,128)(2,1)S(1)} collective-permute-done((bf16[1,4,16,16,128]{4,3,2,1,0:T(8,128)(2,1)S(1)}, bf16[1,4,16,16,128]{4,3,2,1,0:T(8,128)(2,1)S(1)}, u32[]{:S(2)}, u32[]{:S(2)}) %collective-permute-start.1) | collective-permute-done | bytes 262176 | tf_op jit(solution)/shard_map/ppermute | solution.py:14
  94.9 0.3 fusion.287
  97.2 0.3 fusion.288
  99.4 0.3 fusion.22
  100.8 0.3 fusion.54
  103.3 0.3 fusion.36
  103.8 0.3 fusion.34
  105.8 0.3 fusion.27
  108.3 0.3 fusion.45
  108.9 0.3 fusion.43
  109.2 0.3 fusion.42
  110.0 1.6 pad_maximum_fusion
  111.6 19.9 %all-reduce.14.cloned.1.call-done = f32[4,9,128,128]{3,2,1,0:T(8,128)} async-done(((f32[4,9,128,128]{3,2,1,0:T(8,128)}), f32[4,9,128,128]{3,2,1,0:T(8,128)}) %all-reduce.14.cloned.1.call-update) | async-done | bytes 2359312 | tf_op jit(solution)/shard_map/psum | solution.py:104
  131.5 60.8 %all-reduce.15 = bf16[4,9,128,128]{3,2,1,0:T(8,128)(2,1)} all-reduce(f32[4,9,128,128]{3,2,1,0:T(8,128)} %all-reduce.14.cloned.1.call-done), channel_id=1, replica_groups=mesh['groups'=2,'layer'=4,'dp'=2,'chan'=2] {'dp'}, use_global_device_ids=true, to_apply=%region_3.4 | all-reduce | flops 589824 | bytes 3538944 | tf_op jit(solution)/shard_map/psum | solution.py:104
  (108 shorter events, 21.3 us)
Async XLA Ops:
  7.2 13.7 %copy-start.3 = (bf16[1,4,9,128,128]{4,3,2,1,0:T(8,128)(2,1)S(1)}, bf16[1,4,9,128,128]{4,3,2,1,0:T(8,128)(2,1)}, u32[]{:S(2)}) copy-start(bf16[1,4,9,128,128]{4,3,2,1,0:T(8,128)(2,1)} %param.9) | copy-start | bytes 3538948
  7.2 70.8 %all-gather.4.cloned.1.call-start = ((), (), s32[]{:S(2)}) async-start(), calls=%async_computation.1 | async-start | bytes 2621440 | tf_op jit(solution)/shard_map/all_gather | solution.py:21
  7.2 11.6 %collective-permute-start = (bf16[1,4,16,16,128]{4,3,2,1,0:T(8,128)(2,1)}, bf16[1,4,16,16,128]{4,3,2,1,0:T(8,128)(2,1)S(1)}, u32[]{:S(2)}, u32[]{:S(2)}) collective-permute-start(bf16[1,4,16,16,128]{4,3,2,1,0:T(8,128)(2,1)} %param.10), channel_id=1, source_target_pairs={{4,0},{8,4},{12,8},{5,1},{9,5},{13,9},{6,2},{10,6},{14,10},{7,3},{... | collective-permute-start | bytes 786440 | tf_op jit(solution)/shard_map/ppermute | solution.py:14
  22.0 1.2 copy-start
  22.0 1.3 copy-start.2
  29.4 1.0 copy-start.4
  30.4 1.2 copy-start.6
  31.5 100.0 %all-reduce.14.cloned.1.call-start = ((), (), s32[]{:S(2)}) async-start(), calls=%async_computation | async-start | bytes 4718592 | tf_op jit(solution)/shard_map/psum | solution.py:104
  78.0 3.9 %copy-start.1 = (f32[4,16,16,128]{3,2,1,0:T(8,128)S(1)}, f32[4,16,16,128]{3,2,1,0:T(8,128)}, u32[]{:S(2)}) copy-start(f32[4,16,16,128]{3,2,1,0:T(8,128)} %fusion.12) | copy-start | bytes 1572868
  83.0 10.0 %copy-start.5 = (bf16[1,4,16,16,128]{4,3,2,1,0:T(8,128)(2,1)}, bf16[1,4,16,16,128]{4,3,2,1,0:T(8,128)(2,1)S(1)}, u32[]{:S(2)}) copy-start(bf16[1,4,16,16,128]{4,3,2,1,0:T(8,128)(2,1)S(1)} %fusion.62) | copy-start | bytes 786436
  83.0 9.9 %collective-permute-start.1 = (bf16[1,4,16,16,128]{4,3,2,1,0:T(8,128)(2,1)S(1)}, bf16[1,4,16,16,128]{4,3,2,1,0:T(8,128)(2,1)S(1)}, u32[]{:S(2)}, u32[]{:S(2)}) collective-permute-start(bf16[1,4,16,16,128]{4,3,2,1,0:T(8,128)(2,1)S(1)} %fusion.62), channel_id=1, source_target_pairs={{4,0},{8,4},{12,8},{5,1},{9,5},{13,9},{6,2},{10,6},{14,10},{7,3},{... | collective-permute-start | bytes 786440 | tf_op jit(solution)/shard_map/ppermute | solution.py:14
Sparse Core Ops, SparseCore 0:
  31.6 46.3 all-gather.3
  111.8 19.7 all-reduce.13
